TPU v7x, 256 devices: a whole 4x4x8 slice. The times are simulated.
256 devices in a mesh: dp: 2 (over y_hi), fsdp: 8 (over x, y_lo), expert: 16 (over z, core).
Axes of the slice: x: 4, y: 4 (y_hi: 2, y_lo: 2; y = y_hi * 2 + y_lo), z: 8, core: 2. Of those that a mesh axis runs over, the one named last changes fastest.
Arguments:
- tokens: bfloat16 [65536, 2048], P(('dp', 'fsdp', 'expert')), may hold values from -6 to 6
- expert_ids: int32 [65536, 8], P(('dp', 'fsdp', 'expert')), may hold values from 0 to 127, all different within a row; in each aligned block of 256 rows (0 to 255, 256 to 511, ...) at most 24 rows name the same one
- gate_units: int32 [65536, 8], P(('dp', 'fsdp', 'expert')), may hold values from 1 to 256
- expert_weights: bfloat16 [16, 2048, 3, 768], P('expert', ('dp', 'fsdp')), may hold values from -0.125 to 0.125
- out_grad: bfloat16 [65536, 2048], P(('dp', 'fsdp', 'expert')), may hold values from -6 to 6
Outputs:
- moe_out: bfloat16 [65536, 2048], P(('dp', 'fsdp', 'expert'))
- token_grad: bfloat16 [65536, 2048], P(('dp', 'fsdp', 'expert'))
- weight_grad: bfloat16 [16, 2048, 3, 768], P('expert', ('dp', 'fsdp'))
Inputs may be any that keep to these rules, and one draw needn't show every extreme that they name: `expert_ids`: each row names 8 different experts; the 256 rows of one device name one expert at most 24 times.
All inputs are finite; a program needn't handle non-finite values.
Results may differ from a plain program's by a relative error of at most 0.018.
Values may be sent and summed in bfloat16 or wider, within the bound.
A program may use at most 128 MiB of HBM per device.

v0:
```python
import jax
import jax.numpy as jnp
from jax import lax
from jax.sharding import PartitionSpec as P

CAP = 24


def route_tables(expert_ids, gate_units, expert_count, capacity):
    tok_count, top_count = expert_ids.shape
    slot_count = expert_count * capacity
    flat_ids = expert_ids.reshape(tok_count * top_count)
    chosen = (flat_ids[:, None] == jnp.arange(expert_count, dtype=jnp.int32)[None, :]).astype(
        jnp.int32
    )
    before = jnp.cumsum(chosen, axis=0) - chosen
    ranking = jnp.sum(before * chosen, axis=1)
    inside = flat_ids < expert_count
    slot_of = jnp.where(inside, flat_ids * capacity + ranking, slot_count).reshape(
        tok_count, top_count
    )
    matches = slot_of.T[:, None, :] == jnp.arange(slot_count, dtype=jnp.int32)[None, :, None]
    dispatch = jnp.sum(matches.astype(jnp.int32), axis=0).astype(jnp.bfloat16)
    gate_values = gate_units.astype(jnp.float32) / 256.0
    combine = jnp.sum(jnp.where(matches, gate_values.T[:, None, :], 0.0), axis=0)
    return (dispatch, combine)


def on_device(tokens, expert_ids, gate_units, expert_weights, out_grad):
    expert_count = lax.axis_size("expert")
    dispatch, combine = route_tables(expert_ids, gate_units, expert_count, CAP)
    slot_count = expert_count * CAP
    model_width = tokens.shape[1]
    hidden_units = expert_weights.shape[3]
    send_rows = (
        jnp.dot(dispatch, tokens, preferred_element_type=jnp.float32)
        .astype(jnp.bfloat16)
        .reshape(expert_count, CAP, model_width)
    )
    send_grad = (
        jnp.dot(dispatch, out_grad, preferred_element_type=jnp.float32)
        .astype(jnp.bfloat16)
        .reshape(expert_count, CAP, model_width)
    )
    slot_gate = jnp.sum(combine, axis=1).astype(jnp.bfloat16).reshape(expert_count, CAP)
    recv_rows, recv_grad, recv_gate = (
        lax.all_to_all(send_rows, "expert", split_axis=0, concat_axis=0, tiled=True),
        lax.all_to_all(send_grad, "expert", split_axis=0, concat_axis=0, tiled=True),
        lax.all_to_all(slot_gate, "expert", split_axis=0, concat_axis=0, tiled=True),
    )
    full_weights = lax.all_gather(expert_weights, ("dp", "fsdp"), axis=1, tiled=True)
    flat_weights = full_weights.reshape(model_width, 3 * hidden_units)
    slot_rows = recv_rows.reshape(slot_count, model_width)
    gate_up = jnp.dot(
        slot_rows, flat_weights[:, : 2 * hidden_units], preferred_element_type=jnp.float32
    )
    gate_act = gate_up[:, :hidden_units]
    up_act = gate_up[:, hidden_units:]
    sigmoid_gate = jax.nn.sigmoid(gate_act)
    swish_gate = gate_act * sigmoid_gate
    activation = (swish_gate * up_act).astype(jnp.bfloat16)
    down_rows = flat_weights[:, 2 * hidden_units :]
    result = lax.dot_general(
        activation, down_rows, (((1,), (1,)), ((), ())), preferred_element_type=jnp.float32
    ).astype(jnp.bfloat16)
    returned = lax.all_to_all(
        result.reshape(expert_count, CAP, model_width),
        "expert",
        split_axis=0,
        concat_axis=0,
        tiled=True,
    )
    moe_out = lax.dot_general(
        combine.astype(jnp.bfloat16),
        returned.reshape(slot_count, model_width),
        (((0,), (0,)), ((), ())),
        preferred_element_type=jnp.float32,
    ).astype(jnp.bfloat16)
    grad_rows = recv_grad.reshape(slot_count, model_width)
    scaled = (
        recv_gate.reshape(slot_count, 1).astype(jnp.float32) * grad_rows.astype(jnp.float32)
    ).astype(jnp.bfloat16)
    hidden_grad = jnp.dot(scaled, down_rows, preferred_element_type=jnp.float32)
    gate_grad = (
        hidden_grad * up_act * sigmoid_gate * (1.0 + gate_act * (1.0 - sigmoid_gate))
    ).astype(jnp.bfloat16)
    up_grad = (hidden_grad * swish_gate).astype(jnp.bfloat16)
    pair_grad = jnp.concatenate([gate_grad, up_grad], axis=1)
    row_grad = lax.dot_general(
        pair_grad,
        flat_weights[:, : 2 * hidden_units],
        (((1,), (1,)), ((), ())),
        preferred_element_type=jnp.float32,
    ).astype(jnp.bfloat16)
    back_grads = lax.all_to_all(
        row_grad.reshape(expert_count, CAP, model_width),
        "expert",
        split_axis=0,
        concat_axis=0,
        tiled=True,
    )
    token_grad = lax.dot_general(
        dispatch,
        back_grads.reshape(slot_count, model_width),
        (((0,), (0,)), ((), ())),
        preferred_element_type=jnp.float32,
    ).astype(jnp.bfloat16)
    input_term = lax.dot_general(
        slot_rows, pair_grad, (((0,), (0,)), ((), ())), preferred_element_type=jnp.float32
    )
    down_term = lax.dot_general(
        scaled, activation, (((0,), (0,)), ((), ())), preferred_element_type=jnp.float32
    )
    summed = lax.psum_scatter(
        jnp.concatenate([input_term, down_term], axis=1)
        .reshape(lax.axis_size(("dp", "fsdp")) * expert_weights.shape[1], 3, hidden_units)
        .astype(jnp.bfloat16),
        ("dp", "fsdp"),
        scatter_dimension=0,
        tiled=True,
    )
    weight_grad = summed.reshape(expert_weights.shape)
    return (moe_out, token_grad, weight_grad)


def solution(mesh):
    placed = (
        P(("dp", "fsdp", "expert"), None),
        P(("dp", "fsdp", "expert"), None),
        P(("dp", "fsdp", "expert"), None),
        P("expert", ("dp", "fsdp"), None, None),
        P(("dp", "fsdp", "expert"), None),
    )
    return jax.shard_map(
        on_device,
        mesh=mesh,
        in_specs=placed,
        out_specs=(
            P(("dp", "fsdp", "expert"), None),
            P(("dp", "fsdp", "expert"), None),
            P("expert", ("dp", "fsdp"), None, None),
        ),
        check_vma=False,
    )
```

profile of v0, /device:TPU:5, one launch (start us, length us, event | category | flops | bytes accessed | tf_op | source)
XLA Modules:
  0.0 472.6 jit_solution(17774609145026411051)
XLA Ops:
  7.2 2.2 copy.41
  10.5 4.5 reduce-window.6
  17.2 9.2 %all-to-all-start.2 = ((bf16[16,1,24]{2,1,0:T(2,128)(2,1)}), bf16[16,1,24]{2,1,0:T(2,128)(2,1)S(1)}, u32[]{:S(2)}, u32[]{:S(2)}) async-start(bf16[16,1,24]{2,1,0:T(2,128)(2,1)} %convert_element_type.109), calls=%async_computation.2 | async-start | bytes 16384 | tf_op jit(solution)/shard_map/all_to_all | solution.py:49
  28.5 4.8 %all-to-all-done.2 = bf16[16,1,24]{2,1,0:T(2,128)(2,1)S(1)} async-done(((bf16[16,1,24]{2,1,0:T(2,128)(2,1)}), bf16[16,1,24]{2,1,0:T(2,128)(2,1)S(1)}, u32[]{:S(2)}, u32[]{:S(2)}) %all-to-all-start.2) | async-done | bytes 800 | tf_op jit(solution)/shard_map/all_to_all | solution.py:49
  33.3 4.2 all-to-all-start.3
  37.5 2.9 convolution_convert_fusion.4
  40.4 35.5 %all-to-all-done.3 = bf16[16,24,2048]{2,1,0:T(8,128)(2,1)S(1)} async-done(((bf16[16,24,2048]{2,1,0:T(8,128)(2,1)}), bf16[16,24,2048]{2,1,0:T(8,128)(2,1)S(1)}, u32[]{:S(2)}, u32[]{:S(2)}) %all-to-all-start.3) | async-done | bytes 1572896 | tf_op jit(solution)/shard_map/all_to_all | solution.py:48
  76.0 4.3 all-to-all-start
  82.2 36.6 %all-to-all-done = bf16[16,24,2048]{2,1,0:T(8,128)(2,1)} async-done(((bf16[16,24,2048]{2,1,0:T(8,128)(2,1)}), bf16[16,24,2048]{2,1,0:T(8,128)(2,1)}, u32[]{:S(2)}, u32[]{:S(2)}) %all-to-all-start) | async-done | bytes 1572896 | tf_op jit(solution)/shard_map/all_to_all | solution.py:47
  118.8 99.4 %all-gather.2.cloned.1.call-done = bf16[1,2048,3,768]{1,3,2,0:T(8,128)(2,1)} async-done(((bf16[1,128,3,768]{1,3,2,0:T(8,128)(2,1)}), bf16[1,2048,3,768]{1,3,2,0:T(8,128)(2,1)}) %all-gather.2.cloned.1.call-update) | async-done | bytes 9437200 | tf_op jit(solution)/shard_map/all_gather | solution.py:51
  218.2 5.3 %fusion.2 = f32[384,1536]{1,0:T(8,128)S(1)} fusion(bf16[384,2048]{1,0:T(8,128)(2,1)} %bitcast.4, bf16[2048,2304]{0,1:T(8,128)(2,1)} %bitcast.53), kind=kOutput, calls=%fused_computation.4 | convolution fusion | flops 2415919104 | bytes 10223616 | tf_op jit(solution)/shard_map/dot_general | solution.py:54
  223.5 3.7 multiply_convert_fusion.1
  227.3 1.9 convolution_convert_fusion.1
  229.2 5.2 %convolution_convert_fusion = bf16[2048,1536]{0,1:T(8,128)(2,1)S(1)} fusion(bf16[384,2048]{1,0:T(8,128)(2,1)} %bitcast.4, bf16[384,768]{1,0:T(8,128)(2,1)S(1)} %get-tuple-element.6, bf16[384,768]{1,0:T(8,128)(2,1)S(1)} %get-tuple-element.5), kind=kOutput, calls=%fused_computation.1 | convolution fusion | flops 2421424128 | bytes 9043968 | tf_op jit(solution)/shard_map/dot_general | solution.py:108
  234.3 11.5 %pad_maximum_fusion = bf16[2048,2304]{0,1:T(8,128)(2,1)} fusion(bf16[2048,768]{0,1:T(8,128)(2,1)S(1)} %convolution_convert_fusion.1, bf16[2048,1536]{0,1:T(8,128)(2,1)S(1)} %convolution_convert_fusion), kind=kLoop, calls=%fused_computation | loop fusion | flops 18874368 | bytes 18874368 | tf_op jit(solution)/shard_map/concatenate | solution.py:115
  245.9 12.7 %copy.43 = bf16[2048,3,768]{2,0,1:T(8,128)(2,1)} copy(bf16[2048,3,768]{0,2,1:T(8,128)(2,1)} %bitcast.46) | data formatting | bytes 18874368 | tf_op jit(solution)/shard_map/convert_element_type | solution.py:117
  258.6 4.5 convolution_convert_fusion.2
  263.0 11.9 %all-to-all-start.1 = ((bf16[16,24,2048]{2,1,0:T(8,128)(2,1)}), bf16[16,24,2048]{2,1,0:T(8,128)(2,1)S(1)}, u32[]{:S(2)}, u32[]{:S(2)}) async-start(bf16[16,24,2048]{2,1,0:T(8,128)(2,1)} %bitcast.50), calls=%async_computation.1 | async-start | bytes 3145728 | tf_op jit(solution)/shard_map/all_to_all | solution.py:66
  274.9 6.9 %fusion.5 = bf16[384,2048]{1,0:T(8,128)(2,1)} fusion(bf16[2048,2304]{0,1:T(8,128)(2,1)} %bitcast.56, bf16[384,768]{1,0:T(8,128)(2,1)} %copy-done.6, bf16[384,768]{1,0:T(8,128)(2,1)} %copy-done.5), kind=kOutput, calls=%fused_computation.14 | convolution fusion | flops 2419064832 | bytes 9043968 | tf_op jit(solution)/shard_map/dot_general | solution.py:89
  281.8 31.5 %all-to-all-done.1 = bf16[16,24,2048]{2,1,0:T(8,128)(2,1)S(1)} async-done(((bf16[16,24,2048]{2,1,0:T(8,128)(2,1)}), bf16[16,24,2048]{2,1,0:T(8,128)(2,1)S(1)}, u32[]{:S(2)}, u32[]{:S(2)}) %all-to-all-start.1) | async-done | bytes 1572896 | tf_op jit(solution)/shard_map/all_to_all | solution.py:66
  314.5 4.3 all-to-all-start.4
  318.7 3.1 convolution_convert_fusion.6
  321.9 35.3 %all-to-all-done.4 = bf16[16,24,2048]{2,1,0:T(8,128)(2,1)S(1)} async-done(((bf16[16,24,2048]{2,1,0:T(8,128)(2,1)}), bf16[16,24,2048]{2,1,0:T(8,128)(2,1)S(1)}, u32[]{:S(2)}, u32[]{:S(2)}) %all-to-all-start.4) | async-done | bytes 1572896 | tf_op jit(solution)/shard_map/all_to_all | solution.py:95
  358.9 106.9 %reduce-scatter.2.cloned.1.call-done = bf16[128,3,768]{2,0,1:T(8,128)(2,1)} async-done(((bf16[2048,3,768]{2,0,1:T(8,128)(2,1)}), bf16[128,3,768]{2,0,1:T(8,128)(2,1)}) %reduce-scatter.2.cloned.1.call-update) | async-done | bytes 589840 | tf_op jit(solution)/shard_map/reduce_scatter | solution.py:114
  (38 shorter events, 10.1 us)
Async XLA Ops:
  7.2 19.6 %copy-start = (bf16[256,2048]{1,0:T(8,128)(2,1)S(1)}, bf16[256,2048]{1,0:T(8,128)(2,1)}, u32[]{:S(2)}) copy-start(bf16[256,2048]{1,0:T(8,128)(2,1)} %param.9) | copy-start | bytes 3145732
  7.2 8.9 %copy-start.3 = (s32[256,8]{0,1:T(8,128)S(1)}, s32[256,8]{0,1:T(8,128)}, u32[]{:S(2)}) copy-start(s32[256,8]{0,1:T(8,128)} %param.6) | copy-start | bytes 24580
  7.2 8.8 %copy-start.4 = (s32[256,8]{0,1:T(8,128)S(1)}, s32[256,8]{0,1:T(8,128)}, u32[]{:S(2)}) copy-start(s32[256,8]{0,1:T(8,128)} %param.7) | copy-start | bytes 24580
  7.2 211.0 %all-gather.2.cloned.1.call-start = ((), (), s32[]{:S(2)}) async-start(), calls=%async_computation.6 | async-start | bytes 10027008 | tf_op jit(solution)/shard_map/all_gather | solution.py:51
  17.2 16.1 %all-to-all-start.2 = ((bf16[16,1,24]{2,1,0:T(2,128)(2,1)}), bf16[16,1,24]{2,1,0:T(2,128)(2,1)S(1)}, u32[]{:S(2)}, u32[]{:S(2)}) async-start(bf16[16,1,24]{2,1,0:T(2,128)(2,1)} %convert_element_type.109), calls=%async_computation.2 | async-start | bytes 16384 | tf_op jit(solution)/shard_map/all_to_all | solution.py:49
  33.3 42.6 %all-to-all-start.3 = ((bf16[16,24,2048]{2,1,0:T(8,128)(2,1)}), bf16[16,24,2048]{2,1,0:T(8,128)(2,1)S(1)}, u32[]{:S(2)}, u32[]{:S(2)}) async-start(bf16[16,24,2048]{2,1,0:T(8,128)(2,1)} %bitcast.8), calls=%async_computation.3 | async-start | bytes 3145728 | tf_op jit(solution)/shard_map/all_to_all | solution.py:48
  76.0 42.8 %all-to-all-start = ((bf16[16,24,2048]{2,1,0:T(8,128)(2,1)}), bf16[16,24,2048]{2,1,0:T(8,128)(2,1)}, u32[]{:S(2)}, u32[]{:S(2)}) async-start(bf16[16,24,2048]{2,1,0:T(8,128)(2,1)} %bitcast.3), calls=%async_computation | async-start | bytes 3145728 | tf_op jit(solution)/shard_map/all_to_all | solution.py:47
  80.3 385.5 %reduce-scatter.2.cloned.1.call-start = ((), (), s32[]{:S(2)}) async-start(), calls=%async_computation.7 | async-start | bytes 10027008 | tf_op jit(solution)/shard_map/reduce_scatter | solution.py:114
  218.2 5.4 %copy-start.2 = (bf16[384,2048]{1,0:T(8,128)(2,1)S(1)}, bf16[384,2048]{1,0:T(8,128)(2,1)}, u32[]{:S(2)}) copy-start(bf16[384,2048]{1,0:T(8,128)(2,1)} %fusion.4) | copy-start | bytes 4718596
  227.3 1.9 copy-start.5
  227.3 1.9 copy-start.6
  263.0 50.3 %all-to-all-start.1 = ((bf16[16,24,2048]{2,1,0:T(8,128)(2,1)}), bf16[16,24,2048]{2,1,0:T(8,128)(2,1)S(1)}, u32[]{:S(2)}, u32[]{:S(2)}) async-start(bf16[16,24,2048]{2,1,0:T(8,128)(2,1)} %bitcast.50), calls=%async_computation.1 | async-start | bytes 3145728 | tf_op jit(solution)/shard_map/all_to_all | solution.py:66
  313.3 1.2 copy-start.1
  314.5 42.7 %all-to-all-start.4 = ((bf16[16,24,2048]{2,1,0:T(8,128)(2,1)}), bf16[16,24,2048]{2,1,0:T(8,128)(2,1)S(1)}, u32[]{:S(2)}, u32[]{:S(2)}) async-start(bf16[16,24,2048]{2,1,0:T(8,128)(2,1)} %bitcast.49), calls=%async_computation.4 | async-start | bytes 3145728 | tf_op jit(solution)/shard_map/all_to_all | solution.py:95
Sparse Core Ops, SparseCore 0:
  10.3 207.7 all-gather.1
  258.7 207.0 reduce-scatter.1
where the time goes:
time: 474 us; the launch traced here: 473 us
  waiting for transfers between devices  350 us (74%)
  matrix products  37 us (8%)
  starting transfers between devices  34 us (7%)
  other arithmetic  18.8 us (4%)
  local copies, waits for them, and re-layouts  18.5 us (4%)
  between operations  14.2 us (3%)
    reduce_scatter x1, waiting for transfers between devices, on_device(): lax.psum_scatter(jnp.concatenate([input_term, down_term], axis=1).reshape...  107 us
    all_gather x1, waiting for transfers between devices, on_device(): lax.all_gather(expert_weights, ('dp', 'fsdp'), axis=1, tiled=True)  99.4 us
    all_to_all x1, waiting for transfers between devices, on_device(): lax.all_to_all(send_rows, 'expert', split_axis=0, concat_axis=0, tiled=True)  36.6 us
    all_to_all x1, waiting for transfers between devices, on_device(): lax.all_to_all(send_grad, 'expert', split_axis=0, concat_axis=0, tiled=True)  35.5 us
    all_to_all x1, waiting for transfers between devices, on_device(): lax.all_to_all(row_grad.reshape(expert_count, CAP, model_width), 'expert'...  35.3 us
    all_to_all x1, waiting for transfers between devices, on_device(): lax.all_to_all(result.reshape(expert_count, CAP, model_width), 'expert',...  31.5 us
    convert_element_type x1, local copies, waits for them, and re-layouts, on_device(): summed = lax.psum_scatter(jnp.concatenate([input_term, down_term], axis=1...  12.7 us
    all_to_all x1, starting transfers between devices, on_device(): lax.all_to_all(result.reshape(expert_count, CAP, model_width), 'expert',...  11.9 us
  transfers between devices with their start and end apart: 7, of which 7 were waited for; matrix products, arithmetic and copies ran while one was open for 6% of the time, Pallas kernels for 0%

commit v1 on v0

--- a/solution.py
+++ b/solution.py
@@ -48,7 +48,15 @@
         lax.all_to_all(send_grad, "expert", split_axis=0, concat_axis=0, tiled=True),
         lax.all_to_all(slot_gate, "expert", split_axis=0, concat_axis=0, tiled=True),
     )
-    full_weights = lax.all_gather(expert_weights, ("dp", "fsdp"), axis=1, tiled=True)
+    full_weights = jnp.concatenate(
+        lax.all_to_all(
+            jnp.stack(lax.axis_size(("dp", "fsdp")) * [expert_weights], axis=0),
+            ("dp", "fsdp"),
+            0,
+            0,
+        ),
+        axis=1,
+    )
     flat_weights = full_weights.reshape(model_width, 3 * hidden_units)
     slot_rows = recv_rows.reshape(slot_count, model_width)
     gate_up = jnp.dot(

time: 474 us -> 536 us (1.13)
  waiting for transfers between devices: 350 us -> 381 us
  local copies, waits for them, and re-layouts: 18.5 us -> 49.2 us
    all_to_all x0 -> x1, waiting for transfers between devices: none -> 151 us  [on_device(): lax.all_to_all(jnp.stack(lax.axis_size(('dp', 'fsdp')) * [expert_weights]...]
    all_gather x1 -> x0, waiting for transfers between devices: 99.4 us -> none  [on_device(): lax.all_gather(expert_weights, ('dp', 'fsdp'), axis=1, tiled=True)]
    all_to_all x1, waiting for transfers between devices: 36.6 us -> 11.2 us  [on_device(): lax.all_to_all(send_rows, 'expert', split_axis=0, concat_axis=0, tiled=True)]
    all_to_all x0 -> x1, local copies, waits for them, and re-layouts: none -> 13.4 us  [on_device(): lax.all_to_all(jnp.stack(lax.axis_size(('dp', 'fsdp')) * [expert_weights]...]
    unnamed x16 -> x18, local copies, waits for them, and re-layouts: 4.21 us -> 14.2 us
    all_to_all x1, starting transfers between devices: 11.9 us -> 4.38 us  [on_device(): lax.all_to_all(result.reshape(expert_count, CAP, model_width), 'expert',...]
    another operation x0 -> x2, local copies, waits for them, and re-layouts: none -> 7.25 us  [the longest x1 5.88 us: on_device(): jnp.stack(lax.axis_size(('dp', 'fsdp')) * [expert_weights], axis=0)]
    all_to_all x0 -> x1, starting transfers between devices: none -> 7.02 us  [on_device(): lax.all_to_all(jnp.stack(lax.axis_size(('dp', 'fsdp')) * [expert_weights]...]
  transfers between devices with their start and end apart: 7 -> 7, of which waited for: 7 -> 7; matrix products, arithmetic and copies ran while one was open for 6% -> 9% of each run, Pallas kernels for 0% -> 0%
where the time goes in v1:
time: 536 us; the launch traced here: 535 us
  waiting for transfers between devices  381 us (71%)
  local copies, waits for them, and re-layouts  49.2 us (9%)
  matrix products  36.2 us (7%)
  starting transfers between devices  34 us (6%)
  other arithmetic  20.3 us (4%)
  between operations  14.2 us (3%)
    all_to_all x1, waiting for transfers between devices, on_device(): lax.all_to_all(jnp.stack(lax.axis_size(('dp', 'fsdp')) * [expert_weights]...  151 us
    reduce_scatter x1, waiting for transfers between devices, on_device(): lax.psum_scatter(jnp.concatenate([input_term, down_term], axis=1).reshape...  110 us
    all_to_all x1, waiting for transfers between devices, on_device(): lax.all_to_all(send_grad, 'expert', split_axis=0, concat_axis=0, tiled=True)  37.1 us
    all_to_all x1, waiting for transfers between devices, on_device(): lax.all_to_all(row_grad.reshape(expert_count, CAP, model_width), 'expert'...  35.2 us
    all_to_all x1, waiting for transfers between devices, on_device(): lax.all_to_all(result.reshape(expert_count, CAP, model_width), 'expert',...  31.2 us
    unnamed x18, local copies, waits for them, and re-layouts  14.2 us
    all_to_all x1, local copies, waits for them, and re-layouts, on_device(): lax.all_to_all(jnp.stack(lax.axis_size(('dp', 'fsdp')) * [expert_weights]...  13.4 us
    convert_element_type x1, local copies, waits for them, and re-layouts, on_device(): summed = lax.psum_scatter(jnp.concatenate([input_term, down_term], axis=1...  12.7 us
  transfers between devices with their start and end apart: 7, of which 7 were waited for; matrix products, arithmetic and copies ran while one was open for 9% of the time, Pallas kernels for 0%

profile of v1, /device:TPU:5, one launch (start us, length us, event | category | flops | bytes accessed | tf_op | source)
XLA Modules:
  0.0 534.6 jit_solution(2456883741183714704)
XLA Ops:
  8.3 4.5 reduce-window.6
  16.4 9.2 %all-to-all-start.3 = ((bf16[16,1,24]{2,1,0:T(2,128)(2,1)}), bf16[16,1,24]{2,1,0:T(2,128)(2,1)S(1)}, u32[]{:S(2)}, u32[]{:S(2)}) async-start(bf16[16,1,24]{2,1,0:T(2,128)(2,1)} %convert_element_type.109), calls=%async_computation.3 | async-start | bytes 16384 | tf_op jit(solution)/shard_map/all_to_all | solution.py:49
  27.7 4.8 all-to-all-done.3
  32.5 4.2 all-to-all-start.4
  38.0 37.1 %all-to-all-done.4 = bf16[16,24,2048]{2,1,0:T(8,128)(2,1)S(1)} async-done(((bf16[16,24,2048]{2,1,0:T(8,128)(2,1)}), bf16[16,24,2048]{2,1,0:T(8,128)(2,1)S(1)}, u32[]{:S(2)}, u32[]{:S(2)}) %all-to-all-start.4) | async-done | bytes 1572896 | tf_op jit(solution)/shard_map/all_to_all | solution.py:48
  75.1 5.9 %stack.2 = bf16[16,1,128,3,768]{2,4,3,1,0:T(8,128)(2,1)} broadcast(bf16[128,3,768]{0,2,1:T(8,128)(2,1)S(1)} %copy.44), dimensions={2,3,4} | broadcast | bytes 10027008 | tf_op jit(solution)/shard_map/stack | solution.py:53
  81.0 7.0 %all-to-all-start.1 = ((bf16[16,1,128,3,768]{2,4,3,1,0:T(8,128)(2,1)}), bf16[16,1,128,3,768]{2,4,3,1,0:T(8,128)(2,1)}, u32[]{:S(2)}, u32[]{:S(2)}) async-start(bf16[16,1,128,3,768]{2,4,3,1,0:T(8,128)(2,1)} %stack.2), calls=%async_computation.1 | async-start | bytes 18874368 | tf_op jit(solution)/shard_map/all_to_all | solution.py:52
  89.8 151.1 %all-to-all-done.1 = bf16[16,1,128,3,768]{2,4,3,1,0:T(8,128)(2,1)} async-done(((bf16[16,1,128,3,768]{2,4,3,1,0:T(8,128)(2,1)}), bf16[16,1,128,3,768]{2,4,3,1,0:T(8,128)(2,1)}, u32[]{:S(2)}, u32[]{:S(2)}) %all-to-all-start.1) | async-done | bytes 9437216 | tf_op jit(solution)/shard_map/all_to_all | solution.py:52
  240.9 4.8 all-to-all-start
  247.6 13.4 %copy.45 = bf16[16,1,128,3,768]{2,0,4,3,1:T(8,128)(2,1)} copy(bf16[16,1,128,3,768]{2,4,3,1,0:T(8,128)(2,1)} %all-to-all-done.1) | data formatting | bytes 18874368 | tf_op jit(solution)/shard_map/all_to_all | solution.py:52
  261.0 12.1 %copy.52 = bf16[288,8,16,128]{3,1,2,0:T(8,128)(2,1)} copy(bf16[288,8,16,128]{3,2,1,0:T(8,128)(2,1)} %bitcast.54) | data formatting | bytes 18874368
  273.1 11.2 %all-to-all-done = bf16[16,24,2048]{2,1,0:T(8,128)(2,1)} async-done(((bf16[16,24,2048]{2,1,0:T(8,128)(2,1)}), bf16[16,24,2048]{2,1,0:T(8,128)(2,1)}, u32[]{:S(2)}, u32[]{:S(2)}) %all-to-all-start) | async-done | bytes 1572896 | tf_op jit(solution)/shard_map/all_to_all | solution.py:47
  284.3 5.4 %fusion.2 = f32[384,1536]{1,0:T(8,128)S(1)} fusion(bf16[384,2048]{1,0:T(8,128)(2,1)} %bitcast.4, bf16[2048,2304]{0,1:T(8,128)(2,1)} %bitcast.55), kind=kOutput, calls=%fused_computation.5 | convolution fusion | flops 2415919104 | bytes 10223616 | tf_op jit(solution)/shard_map/dot_general | solution.py:62
  289.7 3.7 multiply_convert_fusion.1
  295.3 5.2 convolution_convert_fusion
  300.5 11.5 %pad_maximum_fusion = bf16[2048,2304]{0,1:T(8,128)(2,1)} fusion(bf16[2048,768]{0,1:T(8,128)(2,1)S(1)} %convolution_convert_fusion.1, bf16[2048,1536]{0,1:T(8,128)(2,1)S(1)} %convolution_convert_fusion), kind=kLoop, calls=%fused_computation.1 | loop fusion | flops 18874368 | bytes 18874368 | tf_op jit(solution)/shard_map/concatenate | solution.py:123
  312.0 12.7 %copy.47 = bf16[2048,3,768]{2,0,1:T(8,128)(2,1)} copy(bf16[2048,3,768]{0,2,1:T(8,128)(2,1)} %bitcast.53) | data formatting | bytes 18874368 | tf_op jit(solution)/shard_map/convert_element_type | solution.py:125
  324.8 4.5 convolution_convert_fusion.2
  329.2 4.4 all-to-all-start.2
  333.6 7.2 %fusion.5 = bf16[384,2048]{1,0:T(8,128)(2,1)} fusion(bf16[2048,2304]{0,1:T(8,128)(2,1)} %bitcast.58, bf16[384,768]{1,0:T(8,128)(2,1)} %copy-done.7, bf16[384,768]{1,0:T(8,128)(2,1)S(1)} %copy-done.6), kind=kOutput, calls=%fused_computation.15 | convolution fusion | flops 2419064832 | bytes 9043968 | tf_op jit(solution)/shard_map/dot_general | solution.py:97
  340.8 31.2 %all-to-all-done.2 = bf16[16,24,2048]{2,1,0:T(8,128)(2,1)S(1)} async-done(((bf16[16,24,2048]{2,1,0:T(8,128)(2,1)}), bf16[16,24,2048]{2,1,0:T(8,128)(2,1)S(1)}, u32[]{:S(2)}, u32[]{:S(2)}) %all-to-all-start.2) | async-done | bytes 1572896 | tf_op jit(solution)/shard_map/all_to_all | solution.py:74
  373.2 4.3 all-to-all-start.5
  380.7 35.2 %all-to-all-done.5 = bf16[16,24,2048]{2,1,0:T(8,128)(2,1)S(1)} async-done(((bf16[16,24,2048]{2,1,0:T(8,128)(2,1)}), bf16[16,24,2048]{2,1,0:T(8,128)(2,1)S(1)}, u32[]{:S(2)}, u32[]{:S(2)}) %all-to-all-start.5) | async-done | bytes 1572896 | tf_op jit(solution)/shard_map/all_to_all | solution.py:103
  417.6 110.2 %reduce-scatter.2.cloned.1.call-done = bf16[128,3,768]{2,0,1:T(8,128)(2,1)} async-done(((bf16[2048,3,768]{2,0,1:T(8,128)(2,1)}), bf16[128,3,768]{2,0,1:T(8,128)(2,1)}) %reduce-scatter.2.cloned.1.call-update) | async-done | bytes 589840 | tf_op jit(solution)/shard_map/reduce_scatter | solution.py:122
  (42 shorter events, 19.7 us)
Async XLA Ops:
  7.2 18.8 %copy-start = (bf16[256,2048]{1,0:T(8,128)(2,1)S(1)}, bf16[256,2048]{1,0:T(8,128)(2,1)}, u32[]{:S(2)}) copy-start(bf16[256,2048]{1,0:T(8,128)(2,1)} %param.9) | copy-start | bytes 3145732
  16.4 16.1 %all-to-all-start.3 = ((bf16[16,1,24]{2,1,0:T(2,128)(2,1)}), bf16[16,1,24]{2,1,0:T(2,128)(2,1)S(1)}, u32[]{:S(2)}, u32[]{:S(2)}) async-start(bf16[16,1,24]{2,1,0:T(2,128)(2,1)} %convert_element_type.109), calls=%async_computation.3 | async-start | bytes 16384 | tf_op jit(solution)/shard_map/all_to_all | solution.py:49
  32.5 42.6 %all-to-all-start.4 = ((bf16[16,24,2048]{2,1,0:T(8,128)(2,1)}), bf16[16,24,2048]{2,1,0:T(8,128)(2,1)S(1)}, u32[]{:S(2)}, u32[]{:S(2)}) async-start(bf16[16,24,2048]{2,1,0:T(8,128)(2,1)} %bitcast.8), calls=%async_computation.4 | async-start | bytes 3145728 | tf_op jit(solution)/shard_map/all_to_all | solution.py:48
  81.0 7.0 %copy-start.4 = (bf16[256,2048]{1,0:T(8,128)(2,1)S(1)}, bf16[256,2048]{1,0:T(8,128)(2,1)}, u32[]{:S(2)}) copy-start(bf16[256,2048]{1,0:T(8,128)(2,1)} %param.5) | copy-start | bytes 3145732
  81.0 159.9 %all-to-all-start.1 = ((bf16[16,1,128,3,768]{2,4,3,1,0:T(8,128)(2,1)}), bf16[16,1,128,3,768]{2,4,3,1,0:T(8,128)(2,1)}, u32[]{:S(2)}, u32[]{:S(2)}) async-start(bf16[16,1,128,3,768]{2,4,3,1,0:T(8,128)(2,1)} %stack.2), calls=%async_computation.1 | async-start | bytes 18874368 | tf_op jit(solution)/shard_map/all_to_all | solution.py:52
  240.9 43.4 %all-to-all-start = ((bf16[16,24,2048]{2,1,0:T(8,128)(2,1)}), bf16[16,24,2048]{2,1,0:T(8,128)(2,1)}, u32[]{:S(2)}, u32[]{:S(2)}) async-start(bf16[16,24,2048]{2,1,0:T(8,128)(2,1)} %bitcast.3), calls=%async_computation | async-start | bytes 3145728 | tf_op jit(solution)/shard_map/all_to_all | solution.py:47
  245.7 282.0 %reduce-scatter.2.cloned.1.call-start = ((), (), s32[]{:S(2)}) async-start(), calls=%async_computation.7 | async-start | bytes 10027008 | tf_op jit(solution)/shard_map/reduce_scatter | solution.py:122
  284.3 5.4 %copy-start.3 = (bf16[384,2048]{1,0:T(8,128)(2,1)S(1)}, bf16[384,2048]{1,0:T(8,128)(2,1)}, u32[]{:S(2)}) copy-start(bf16[384,2048]{1,0:T(8,128)(2,1)} %fusion.4) | copy-start | bytes 4718596
  293.4 1.9 copy-start.5
  293.4 1.9 copy-start.7
  329.2 4.4 copy-start.6
  329.2 42.8 %all-to-all-start.2 = ((bf16[16,24,2048]{2,1,0:T(8,128)(2,1)}), bf16[16,24,2048]{2,1,0:T(8,128)(2,1)S(1)}, u32[]{:S(2)}, u32[]{:S(2)}) async-start(bf16[16,24,2048]{2,1,0:T(8,128)(2,1)} %bitcast.62), calls=%async_computation.2 | async-start | bytes 3145728 | tf_op jit(solution)/shard_map/all_to_all | solution.py:74
  372.0 1.2 copy-start.2
  373.2 42.7 %all-to-all-start.5 = ((bf16[16,24,2048]{2,1,0:T(8,128)(2,1)}), bf16[16,24,2048]{2,1,0:T(8,128)(2,1)S(1)}, u32[]{:S(2)}, u32[]{:S(2)}) async-start(bf16[16,24,2048]{2,1,0:T(8,128)(2,1)} %bitcast.61), calls=%async_computation.5 | async-start | bytes 3145728 | tf_op jit(solution)/shard_map/all_to_all | solution.py:103
  377.4 150.3 %copy-start.1 = (bf16[256,2048]{1,0:T(8,128)(2,1)S(1)}, bf16[256,2048]{1,0:T(8,128)(2,1)}, u32[]{:S(2)}) copy-start(bf16[256,2048]{1,0:T(8,128)(2,1)} %param.9) | copy-start | bytes 3145732
Sparse Core Ops, SparseCore 0:
  324.9 202.8 reduce-scatter.1
